TPU v7x, 256 devices: a whole 4x4x8 slice. The times are simulated.
256 devices in a mesh: ctx: 32 (over y_lo, z, core), head: 8 (over y_hi, x).
Axes of the slice: x: 4, y: 4 (y_hi: 2, y_lo: 2; y = y_hi * 2 + y_lo), z: 8, core: 2. Of those that a mesh axis runs over, the one named last changes fastest.
Arguments:
- queries: bfloat16 [4096, 2048], P('ctx', 'head'), may hold values from -6 to 6
- key_states: bfloat16 [4096, 2048], P('ctx', 'head'), may hold values from -6 to 6
- value_states: bfloat16 [4096, 2048], P('ctx', 'head'), may hold values from -6 to 6
- memory_keys: bfloat16 [1024, 2048], P('ctx', 'head'), may hold values from -6 to 6
- memory_values: bfloat16 [1024, 2048], P('ctx', 'head'), may hold values from -6 to 6
- memory_length: int32 [32], replicated, may hold values from 256 to 1024, as said below
- block_mask: int32 [32, 32], replicated, may hold values from 0 to 1, as said below
- out_weight: bfloat16 [2048, 4096], P('head'), may hold values from -0.125 to 0.125
- out_grad: bfloat16 [4096, 4096], P('ctx'), may hold values from -6 to 6
Outputs:
- layer_out: bfloat16 [4096, 4096], P('ctx', 'head')
- grad_weight: bfloat16 [2048, 4096], P('head', 'ctx')
- grad_queries: bfloat16 [4096, 2048], P('ctx', 'head')
- grad_keys: bfloat16 [4096, 2048], P('ctx', 'head')
- grad_values: bfloat16 [4096, 2048], P('ctx', 'head')
Inputs may be any that keep to these rules, and one draw needn't show every extreme that they name: `memory_length`: at least 256; some block sees all 1024. `block_mask`: 0 or 1; every diagonal entry is 1.
All inputs are finite; a program needn't handle non-finite values.
Results may differ from a plain program's by a relative error of at most 0.03.
Values may be sent and summed in bfloat16 or wider, within the bound.
A program may use at most 128 MiB of HBM per device.

v0:
```python
import math

import jax
import jax.numpy as jnp
from jax import lax
from jax.sharding import PartitionSpec as P

HD = 128
BLK = 128


def block_allow(block_mask, query_start, query_rows, key_start, key_rows):
    blocks = (
        lax.dynamic_slice(
            block_mask, (query_start // BLK, key_start // BLK), (query_rows // BLK, key_rows // BLK)
        )
        > 0
    )
    allow = jnp.repeat(jnp.repeat(blocks, BLK, axis=0), BLK, axis=1)
    return (blocks, allow)


def head_scores(query_heads, key_heads, scale):
    return (
        jnp.einsum("qhd,khd->hqk", query_heads, key_heads, preferred_element_type=jnp.float32)
        * scale
    )


def absorb(state, scores, allow, value_heads):
    top, total, accum = state
    scores = jnp.where(allow[None], scores, -jnp.inf)
    new_top = jnp.maximum(top, jnp.max(scores, axis=2))
    fade = jnp.exp(top - new_top)
    weights = jnp.exp(scores - new_top[:, :, None])
    total = total * fade + jnp.sum(weights, axis=2)
    accum = accum * fade[:, :, None] + jnp.einsum(
        "hqk,khd->hqd",
        weights,
        value_heads.astype(jnp.float32),
        precision=lax.Precision.HIGHEST,
        preferred_element_type=jnp.float32,
    )
    return (new_top, total, accum)


def tile_grads(query_heads, grad_heads, lse_rows, delta_rows, key_heads, value_heads, allow, scale):
    scores = head_scores(query_heads, key_heads, scale)
    probs = jnp.where(allow[None], jnp.exp(scores - lse_rows[:, :, None]), 0.0)
    grad_probs = jnp.einsum(
        "qhd,khd->hqk", grad_heads, value_heads, preferred_element_type=jnp.float32
    )
    grad_scores = (probs * (grad_probs - delta_rows[:, :, None])).astype(jnp.bfloat16)
    grad_q = jnp.einsum("hqk,khd->qhd", grad_scores, key_heads, preferred_element_type=jnp.float32)
    grad_k = jnp.einsum(
        "hqk,qhd->khd", grad_scores, query_heads, preferred_element_type=jnp.float32
    )
    grad_v = jnp.einsum(
        "hqk,qhd->khd", probs.astype(jnp.bfloat16), grad_heads, preferred_element_type=jnp.float32
    )
    return (grad_q, grad_k, grad_v)


def per_device(
    queries,
    key_states,
    value_states,
    memory_keys,
    memory_values,
    memory_length,
    block_mask,
    out_weight,
    out_grad,
):
    rows_own = queries.shape[0]
    heads = queries.shape[1] // HD
    scale = 1.0 / math.sqrt(HD)
    position = lax.axis_index("ctx")
    query_start = position * rows_own
    query_heads = queries.reshape(rows_own, heads, HD)
    mem_keys, mem_values = (
        lax.all_gather(memory_keys, "ctx", axis=0, tiled=True),
        lax.all_gather(memory_values, "ctx", axis=0, tiled=True),
    )
    mem_rows = mem_keys.shape[0]
    mem_key_heads = mem_keys.reshape(mem_rows, heads, HD)
    mem_value_heads = mem_values.reshape(mem_rows, heads, HD)
    own_length = jnp.repeat(
        lax.dynamic_slice_in_dim(memory_length, query_start // BLK, rows_own // BLK), BLK
    )
    mem_allow = jnp.arange(mem_rows)[None, :] < own_length[:, None]
    mem_scores = head_scores(query_heads, mem_key_heads, scale)
    initial = (
        jnp.full((heads, rows_own), -jnp.inf, jnp.float32),
        jnp.zeros((heads, rows_own), jnp.float32),
        jnp.zeros((heads, rows_own, HD), jnp.float32),
    )
    state = absorb(initial, mem_scores, mem_allow, mem_value_heads)
    key_piece = lax.all_gather(key_states, "ctx", axis=0, tiled=True)
    value_piece = lax.all_gather(value_states, "ctx", axis=0, tiled=True)
    piece_rows = key_piece.shape[0]
    blocks, allow = block_allow(block_mask, query_start, rows_own, jnp.int32(0), piece_rows)
    key_piece_heads = key_piece.reshape(piece_rows, heads, HD)
    value_piece_heads = value_piece.reshape(piece_rows, heads, HD)
    top, total, accum = absorb(
        state, head_scores(query_heads, key_piece_heads, scale), allow, value_piece_heads
    )
    lse = top + jnp.log(total)
    attended = (
        (accum / total[:, :, None])
        .transpose(1, 0, 2)
        .reshape(rows_own, heads * HD)
        .astype(jnp.bfloat16)
    )
    att_heads = attended.reshape(rows_own, heads, HD)
    partial_out = jnp.dot(attended, out_weight, preferred_element_type=jnp.float32)
    layer_out = lax.psum_scatter(partial_out, "head", scatter_dimension=1, tiled=True).astype(
        jnp.bfloat16
    )
    weight_rows = lax.psum_scatter(
        lax.dot_general(
            out_grad, attended, (((0,), (0,)), ((), ())), preferred_element_type=jnp.float32
        ),
        "ctx",
        scatter_dimension=0,
        tiled=True,
    )
    grad_weight = weight_rows.T.astype(jnp.bfloat16)
    grad_att = lax.dot_general(
        out_grad, out_weight, (((1,), (1,)), ((), ())), preferred_element_type=jnp.float32
    ).astype(jnp.bfloat16)
    grad_heads = grad_att.reshape(rows_own, heads, HD)
    delta = jnp.einsum("qhd,qhd->hq", grad_heads, att_heads, preferred_element_type=jnp.float32)
    mem_probs = jnp.where(mem_allow[None], jnp.exp(mem_scores - lse[:, :, None]), 0.0)
    mem_grad_probs = jnp.einsum(
        "qhd,khd->hqk", grad_heads, mem_value_heads, preferred_element_type=jnp.float32
    )
    mem_grad_scores = (mem_probs * (mem_grad_probs - delta[:, :, None])).astype(jnp.bfloat16)
    grad_q_memory = jnp.einsum(
        "hqk,khd->qhd", mem_grad_scores, mem_key_heads, preferred_element_type=jnp.float32
    )
    key_piece = lax.all_gather(key_states, "ctx", axis=0, tiled=True)
    value_piece = lax.all_gather(value_states, "ctx", axis=0, tiled=True)
    piece_rows = key_piece.shape[0]
    blocks, allow = block_allow(block_mask, query_start, rows_own, jnp.int32(0), piece_rows)
    key_piece_heads = key_piece.reshape(piece_rows, heads, HD)
    value_piece_heads = value_piece.reshape(piece_rows, heads, HD)
    grad_q, grad_k, grad_v = tile_grads(
        query_heads, grad_heads, lse, delta, key_piece_heads, value_piece_heads, allow, scale
    )
    grad_k_sum, grad_v_sum = (
        lax.psum_scatter(grad_k, "ctx", scatter_dimension=0, tiled=True),
        lax.psum_scatter(grad_v, "ctx", scatter_dimension=0, tiled=True),
    )
    grad_queries = (
        ((grad_q + grad_q_memory) * scale).reshape(rows_own, heads * HD).astype(jnp.bfloat16)
    )
    grad_keys = (grad_k_sum * scale).reshape(rows_own, heads * HD).astype(jnp.bfloat16)
    grad_values = grad_v_sum.reshape(rows_own, heads * HD).astype(jnp.bfloat16)
    return (layer_out, grad_weight, grad_queries, grad_keys, grad_values)


def solution(mesh):
    in_specs = (
        P("ctx", "head"),
        P("ctx", "head"),
        P("ctx", "head"),
        P("ctx", "head"),
        P("ctx", "head"),
        P(),
        P(),
        P("head", None),
        P("ctx", None),
    )
    out_specs = (
        P("ctx", "head"),
        P("head", "ctx"),
        P("ctx", "head"),
        P("ctx", "head"),
        P("ctx", "head"),
    )
    return jax.shard_map(
        per_device, mesh=mesh, in_specs=in_specs, out_specs=out_specs, check_vma=False
    )
```

profile of v0, /device:TPU:4, one launch (start us, length us, event | category | flops | bytes accessed | tf_op | source)
XLA Modules:
  0.0 611.8 jit_solution(9618610954056185198)
XLA Ops:
  7.3 1.7 copy.48
  9.0 0.0 all-gather.5.cloned.1.call-start
  9.0 0.7 all-gather.5.cloned.1.call-update
  9.7 0.0 reduce-scatter.5.cloned.1.call-start
  9.8 2.1 convolution_convert_fusion
  12.0 0.8 copy.71
  12.7 39.0 %all_gather.14 = bf16[1024,256]{1,0:T(8,128)(2,1)S(1)} all-gather(bf16[32,256]{1,0:T(8,128)(2,1)} %param.12), channel_id=1, replica_groups=mesh['ctx'=32,'head'=8] {'ctx'}, dimensions={0}, use_global_device_ids=true | all-gather | bytes 540672 | tf_op jit(solution)/shard_map/all_gather | solution.py:82
  51.7 1.0 copy.44
  52.7 32.1 %all_gather.15 = bf16[1024,256]{1,0:T(8,128)(2,1)S(1)} all-gather(bf16[32,256]{1,0:T(8,128)(2,1)S(1)} %copy-done.9), channel_id=1, replica_groups=mesh['ctx'=32,'head'=8] {'ctx'}, dimensions={0}, use_global_device_ids=true | all-gather | bytes 540672 | tf_op jit(solution)/shard_map/all_gather | solution.py:83
  84.8 1.0 copy.47
  85.8 0.6 dynamic_slice.10
  86.4 0.7 compare_bitcast_fusion
  87.1 0.7 iota_compare_fusion
  87.8 1.4 select_reduce_fusion.1
  89.3 0.3 fusion.27
  89.6 0.1 broadcast_bitcast_fusion
  89.7 2.5 select_reduce_fusion
  92.2 1.9 copy-done.1
  94.2 0.9 fusion.2
  95.1 49.8 %all-gather.5.cloned.1.call-done = bf16[4096,256]{1,0:T(8,128)(2,1)} async-done(((bf16[128,256]{1,0:T(8,128)(2,1)}), bf16[4096,256]{1,0:T(8,128)(2,1)}) %all-gather.5.cloned.1.call-update) | async-done | bytes 2097168 | tf_op jit(solution)/shard_map/all_gather | solution.py:100
  144.8 4.1 copy.51
  148.9 5.7 fusion.17
  154.7 1.5 multiply_reduce_fusion
  156.2 1.8 fusion.50
  158.0 0.0 reduce-scatter.11.cloned.1.call-start
  158.1 0.1 copy.59
  158.2 4.9 convolution_bitcast_fusion
  163.2 0.2 reduce-scatter.9.cloned.1.call-start
  163.4 0.4 copy-done.14
  163.8 4.2 fusion.1
  168.0 1.3 copy-done.2
  169.3 2.9 convolution_bitcast_fusion.1
  172.3 0.0 reduce-scatter.7.cloned.1.call-start
  172.3 2.7 convolution_bitcast_fusion.2
  175.0 3.0 fusion.51
  178.1 1.9 fusion.23
  179.9 0.7 copy.60
  180.7 56.3 %reduce-scatter.5.cloned.1.call-done = f32[128,512]{1,0:T(8,128)} async-done(((f32[128,4096]{1,0:T(8,128)}), f32[128,512]{1,0:T(8,128)}) %reduce-scatter.5.cloned.1.call-update) | async-done | bytes 262160 | tf_op jit(solution)/shard_map/reduce_scatter | solution.py:117
  237.0 1.6 convert_element_type.53
  238.6 123.5 %reduce-scatter.11.cloned.1.call-done = f32[128,2,128]{0,2,1:T(8,128)} async-done(((f32[4096,2,128]{0,2,1:T(8,128)}), f32[128,2,128]{0,2,1:T(8,128)}) %reduce-scatter.11.cloned.1.call-update) | async-done | bytes 131088 | tf_op jit(solution)/shard_map/reduce_scatter | solution.py:153
  362.1 0.9 convert_element_type.65
  363.1 0.7 copy.62
  363.8 119.0 %reduce-scatter.9.cloned.1.call-done = f32[128,2,128]{2,0,1:T(8,128)} async-done(((f32[4096,2,128]{2,0,1:T(8,128)}), f32[128,2,128]{2,0,1:T(8,128)}) %reduce-scatter.9.cloned.1.call-update) | async-done | bytes 131088 | tf_op jit(solution)/shard_map/reduce_scatter | solution.py:152
  482.8 0.9 multiply_convert_fusion
  483.7 0.1 copy.58
  483.8 0.7 copy.61
  484.6 118.9 %reduce-scatter.7.cloned.1.call-done = f32[128,256]{0,1:T(8,128)} async-done(((f32[4096,256]{0,1:T(8,128)}), f32[128,256]{0,1:T(8,128)}) %reduce-scatter.7.cloned.1.call-update) | async-done | bytes 131088 | tf_op jit(solution)/shard_map/reduce_scatter | solution.py:120
  603.5 1.5 convert_bitcast_fusion
  (41 shorter events, 0.3 us)
Async XLA Ops:
  7.2 2.6 copy-start
  7.2 45.5 %copy-start.9 = (bf16[32,256]{1,0:T(8,128)(2,1)S(1)}, bf16[32,256]{1,0:T(8,128)(2,1)}, u32[]{:S(2)}) copy-start(bf16[32,256]{1,0:T(8,128)(2,1)} %param.13) | copy-start | bytes 49156
  7.2 78.7 %copy-start.15 = (s32[32]{0:T(128)S(1)}, s32[32]{0:T(128)}, u32[]{:S(2)}) copy-start(s32[32]{0:T(128)} %param.14) | copy-start | bytes 388
  7.2 80.6 %copy-start.6 = (bf16[128,256]{1,0:T(8,128)(2,1)S(1)}, bf16[128,256]{1,0:T(8,128)(2,1)}, u32[]{:S(2)}) copy-start(bf16[128,256]{1,0:T(8,128)(2,1)} %param.9) | copy-start | bytes 196612
  7.2 82.5 %all-gather.3.cloned.1.call-start = ((), (), s32[]{:S(2)}) async-start(), calls=%async_computation.4 | async-start | bytes 2162688 | tf_op jit(solution)/shard_map/all_gather | solution.py:99
  9.0 135.9 %all-gather.5.cloned.1.call-start = ((), (), s32[]{:S(2)}) async-start(), calls=%async_computation.5 | async-start | bytes 2162688 | tf_op jit(solution)/shard_map/all_gather | solution.py:100
  9.7 227.2 %reduce-scatter.5.cloned.1.call-start = ((), (), s32[]{:S(2)}) async-start(), calls=%async_computation.6 | async-start | bytes 2359296 | tf_op jit(solution)/shard_map/reduce_scatter | solution.py:117
  89.3 65.4 %copy-start.4 = (f32[2,128,1024]{2,1,0:T(8,128)}, f32[2,128,1024]{2,1,0:T(8,128)S(1)}, u32[]{:S(2)}) copy-start(f32[2,128,1024]{2,1,0:T(8,128)S(1)} %get-tuple-element.24) | copy-start | bytes 3145732
  92.2 2.0 copy-start.1
  92.2 56.7 %copy-start.10 = (f32[2,128]{1,0:T(2,128)}, f32[2,128]{1,0:T(2,128)S(1)}, u32[]{:S(2)}) copy-start(f32[2,128]{1,0:T(2,128)S(1)} %max.21) | copy-start | bytes 3076
  95.1 59.6 %copy-start.12 = (f32[2,128]{1,0:T(2,128)}, f32[2,128]{1,0:T(2,128)S(1)}, u32[]{:S(2)}) copy-start(f32[2,128]{1,0:T(2,128)S(1)} %fusion.2) | copy-start | bytes 3076
  148.9 5.8 copy-start.7
  148.9 5.8 copy-start.8
  156.2 2.0 copy-start.11
  156.2 2.0 copy-start.13
  158.0 204.1 %reduce-scatter.11.cloned.1.call-start = ((), (), s32[]{:S(2)}) async-start(), calls=%async_computation.9 | async-start | bytes 4325376 | tf_op jit(solution)/shard_map/reduce_scatter | solution.py:153
  163.2 0.7 copy-start.14
  163.2 319.6 %reduce-scatter.9.cloned.1.call-start = ((), (), s32[]{:S(2)}) async-start(), calls=%async_computation.8 | async-start | bytes 4325376 | tf_op jit(solution)/shard_map/reduce_scatter | solution.py:152
  168.0 1.3 copy-start.2
  169.3 3.0 copy-start.3
  172.3 431.2 %reduce-scatter.7.cloned.1.call-start = ((), (), s32[]{:S(2)}) async-start(), calls=%async_computation.7 | async-start | bytes 4325376 | tf_op jit(solution)/shard_map/reduce_scatter | solution.py:120
  175.0 3.1 copy-start.5
Sparse Core Ops, SparseCore 0:
  10.4 69.2 all-gather.2
  81.5 63.2 all-gather.4
  158.1 78.7 reduce-scatter.4
  239.5 122.5 reduce-scatter.10
  364.7 118.0 reduce-scatter.8
  485.3 118.0 reduce-scatter.6
where the time goes:
time: 612 us
  waiting for transfers between devices  468 us (76%)
  blocking collectives  71.1 us (12%)
  matrix products  34.6 us (6%)
  local copies, waits for them, and re-layouts  15.5 us (3%)
  between operations  14.4 us (2%)
  other arithmetic  7.69 us (1%)
    reduce_scatter x1, waiting for transfers between devices, per_device(): lax.psum_scatter(grad_v, 'ctx', scatter_dimension=0, tiled=True)  124 us
    reduce_scatter x1, waiting for transfers between devices, per_device(): lax.psum_scatter(grad_k, 'ctx', scatter_dimension=0, tiled=True)  119 us
    reduce_scatter x1, waiting for transfers between devices, per_device(): lax.psum_scatter(lax.dot_general(out_grad, attended, (((0,), (0,)), ((),...  119 us
    reduce_scatter x1, waiting for transfers between devices, per_device(): lax.psum_scatter(partial_out, 'head', scatter_dimension=1, tiled=True)  56.3 us
    all_gather x1, waiting for transfers between devices, per_device(): value_piece = lax.all_gather(value_states, 'ctx', axis=0, tiled=True)  49.8 us
    all_gather x1, blocking collectives, per_device(): lax.all_gather(memory_keys, 'ctx', axis=0, tiled=True)  39 us
    all_gather x1, blocking collectives, per_device(): lax.all_gather(memory_values, 'ctx', axis=0, tiled=True)  32.1 us
  transfers between devices with their start and end apart: 6, of which 5 were waited for; matrix products, arithmetic and copies ran while one was open for 6% of the time, Pallas kernels for 0%

commit v1 on v0

v1 whole, which is shorter than its diff:
```python
import functools
import math

import jax
import jax.numpy as jnp
from jax import lax
from jax.experimental import pallas as pl
from jax.experimental.pallas import tpu as pltpu
from jax.sharding import PartitionSpec as P

HD = 128
BLK = 128
NZ = 8
F32 = jnp.float32
BF16 = jnp.bfloat16
MESH = pl.DeviceIdType.MESH
LOG2E = 1.4426950408889634

OFFSET = (0, -1, 1, -2, 2, -3, 3, 4)
SLOT_OF = {off % NZ: slot for slot, off in enumerate(OFFSET)}

K0, V0, MK0, MV0, ROWS1 = 0, 128, 256, 288, 320
Q0, D0, ROWS2 = 0, 128, 256


def dot_nt(a, b):
    return lax.dot_general(a, b, (((1,), (1,)), ((), ())), preferred_element_type=F32)


def dot_nn(a, b):
    return lax.dot_general(a, b, (((1,), (0,)), ((), ())), preferred_element_type=F32)


def kernel(
    heads_n,
    len_ref,
    mask_ref,
    q_hbm,
    k_hbm,
    v_hbm,
    mk_hbm,
    mv_hbm,
    w_hbm,
    og_hbm,
    lo_out,
    gw_out,
    gq_out,
    gk_out,
    gv_out,
    g1,
    g2,
    s_buf,
    w_buf,
    og_buf,
    ogx,
    do_scr,
    o_scr,
    on_scr,
    att_scr,
    ld,
    lo_own,
    lo_send,
    lo_recv,
    gs_send,
    gs_recv,
    gw_acc,
    gw_send,
    gw_recv,
    m_scr,
    l_scr,
    acc_scr,
    dq_scr,
    dk_scr,
    dv_scr,
    grads,
    lo_stage,
    gw_stage,
    local_sem,
    ring_ss,
    ring_rs,
    sib_ss,
    sib_rs,
    y_ss,
    y_rs,
    ld_ss,
    ld_rs,
    lo_ss,
    lo_rs,
    gw_ss,
    gw_rs,
    out_sem,
):
    ctx = lax.axis_index("ctx")
    head = lax.axis_index("head")
    core = lax.rem(ctx, 2)
    z = lax.rem(ctx // 2, NZ)
    i = ctx // (2 * NZ)
    scale = 1.0 / math.sqrt(HD)

    def at(ii, zz, cc):
        return {"ctx": (ii * NZ + zz) * 2 + cc}

    def z_at(off):
        return lax.rem(z + (off % NZ), NZ)

    y_dev = at(1 - i, z, core)
    sib_dev = at(i, z, 1 - core)
    own_cols = pl.ds(pl.multiple_of(i * HD, HD), HD)
    other_cols = pl.ds(pl.multiple_of((1 - i) * HD, HD), HD)
    gather = (g1, g2)
    started = []

    def remote(src, dst, ss, rs, dev):
        return pltpu.make_async_remote_copy(
            src_ref=src, dst_ref=dst, send_sem=ss, recv_sem=rs, device_id=dev, device_id_type=MESH
        )

    def go(copy):
        copy.start()
        started.append(copy)
        return copy

    piece = g1.at[0, 0, 0]
    local1 = [
        pltpu.make_async_copy(k_hbm.at[:, own_cols], piece.at[K0 : K0 + 128], local_sem.at[0]),
        pltpu.make_async_copy(v_hbm.at[:, own_cols], piece.at[V0 : V0 + 128], local_sem.at[1]),
        pltpu.make_async_copy(mk_hbm.at[:, own_cols], piece.at[MK0 : MK0 + 32], local_sem.at[2]),
        pltpu.make_async_copy(mv_hbm.at[:, own_cols], piece.at[MV0 : MV0 + 32], local_sem.at[3]),
    ]
    local_q = pltpu.make_async_copy(
        q_hbm.at[:, own_cols], g2.at[0, 0, 0, Q0 : Q0 + 128], local_sem.at[4]
    )
    local_w = pltpu.make_async_copy(w_hbm, w_buf, local_sem.at[5])
    local_og = pltpu.make_async_copy(og_hbm, og_buf, local_sem.at[6])
    for copy in local1:
        copy.start()
    local_q.start()
    local_og.start()
    local_w.start()

    barrier = pltpu.get_barrier_semaphore()
    peers = [y_dev, sib_dev]
    peers += [at(i, z_at(off), core) for off in range(1, NZ)]
    peers += [{"head": lax.rem(head + k, heads_n)} for k in range(1, heads_n)]
    for dev in peers:
        pl.semaphore_signal(barrier, inc=1, device_id=dev, device_id_type=MESH)
    pl.semaphore_wait(barrier, len(peers))

    far = g1.at[0, 0, 1]
    y_first = [
        remote(k_hbm.at[:, other_cols], far.at[K0 : K0 + 128], y_ss.at[0], y_rs.at[0], y_dev),
        remote(v_hbm.at[:, other_cols], far.at[V0 : V0 + 128], y_ss.at[1], y_rs.at[1], y_dev),
        remote(mk_hbm.at[:, other_cols], far.at[MK0 : MK0 + 32], y_ss.at[2], y_rs.at[2], y_dev),
        remote(mv_hbm.at[:, other_cols], far.at[MV0 : MV0 + 32], y_ss.at[3], y_rs.at[3], y_dev),
    ]
    y_q = remote(
        q_hbm.at[:, other_cols], g2.at[0, 0, 1, Q0 : Q0 + 128], y_ss.at[4], y_rs.at[4], y_dev
    )
    for copy in y_first:
        go(copy)
    go(y_q)

    def ring(phase, way, step, part):
        src = 0 if step == 0 else 2 * step - 1 + way
        dst = 7 if step == 3 else 2 * step + 1 + way
        buf = gather[phase]
        return remote(
            buf.at[0, src, part],
            buf.at[0, dst, part],
            ring_ss.at[phase, way, step, part],
            ring_rs.at[phase, way, step, part],
            at(i, z_at(1 if way == 0 else -1), core),
        )

    def ring_send(phase, step, part):
        for way in (0, 1):
            if step < 3 or part == way:
                go(ring(phase, way, step, part))

    def sib(phase, slot):
        buf = gather[phase]
        return remote(
            buf.at[0, slot], buf.at[1, slot], sib_ss.at[phase, slot], sib_rs.at[phase, slot], sib_dev
        )

    def advance(phase, step):
        if step < 3:
            for part in (0, 1):
                for way in (0, 1):
                    ring(phase, way, step, part).wait_recv()
                ring_send(phase, step + 1, part)
            go(sib(phase, 2 * step + 1))
            go(sib(phase, 2 * step + 2))
        else:
            ring(phase, 0, 3, 0).wait_recv()
            ring(phase, 1, 3, 1).wait_recv()
            go(sib(phase, 7))

    for copy in local1:
        copy.wait()
    ring_send(0, 0, 0)
    for copy in y_first:
        copy.wait_recv()
    ring_send(0, 0, 1)
    go(sib(0, 0))

    local_og.wait()
    local_w.wait()
    grad_att = dot_nt(og_buf[...], w_buf[...]).astype(BF16)
    do_scr[0] = grad_att[:, :HD]
    do_scr[1] = grad_att[:, HD:]
    g2[0, 0, 0, D0 : D0 + 128, :] = do_scr[i]
    y_do = go(
        remote(do_scr.at[1 - i], g2.at[0, 0, 1, D0 : D0 + 128], y_ss.at[5], y_rs.at[5], y_dev)
    )
    half = og_hbm.shape[1] // 2
    y_og = go(
        remote(
            og_hbm.at[:, pl.ds(pl.multiple_of((1 - i) * half, HD), half)],
            ogx,
            y_ss.at[6],
            y_rs.at[6],
            y_dev,
        )
    )
    local_q.wait()
    y_q.wait_recv()

    def block_of(part, slot, crel):
        ii = i if part == 0 else 1 - i
        cc = core if crel == 0 else 1 - core
        return (ii * NZ + z_at(OFFSET[slot])) * 2 + cc

    own_blocks = [block_of(0, 0, 0), block_of(1, 0, 0)]

    def both(buf, crel, slot, row, rows):
        return jnp.concatenate(
            [buf[crel, slot, 0, row : row + rows, :], buf[crel, slot, 1, row : row + rows, :]], axis=0
        )

    q_mine = both(g2, 0, 0, Q0, 128)
    m_scr[...] = jnp.full_like(m_scr, -jnp.inf)
    l_scr[...] = jnp.zeros_like(l_scr)
    acc_scr[...] = jnp.zeros_like(acc_scr)
    lane = lax.broadcasted_iota(jnp.int32, (1, 256), 1)

    def seq_scores(crel, slot):
        s = dot_nt(q_mine, both(g1, crel, slot, K0, 128)) * (scale * LOG2E)
        top = None
        for yq in (0, 1):
            row = []
            for yk in (0, 1):
                bias = jnp.where(
                    mask_ref[own_blocks[yq], block_of(yk, slot, crel)] > 0, 0.0, -jnp.inf
                )
                row.append(s[yq * 128 : yq * 128 + 128, yk * 128 : yk * 128 + 128] + bias)
                s_buf[crel * 8 + slot, yq * 128 : yq * 128 + 128, yk * 128 : yk * 128 + 128] = row[yk]
            both_k = jnp.maximum(row[0], row[1])
            top = both_k if top is None else jnp.concatenate([top, both_k], axis=0)
        return top

    def mem_rows(crel, group, row):
        return jnp.concatenate(
            [
                g1[crel, slot, part, row : row + 32, :]
                for slot in range(4 * group, 4 * group + 4)
                for part in (0, 1)
            ],
            axis=0,
        )

    def mem_scores(crel, group):
        s = dot_nt(q_mine, mem_rows(crel, group, MK0)) * (scale * LOG2E)
        base = jnp.zeros((1, 256), jnp.int32)
        place = 0
        for slot in range(4 * group, 4 * group + 4):
            for part in (0, 1):
                base = jnp.where(lane // 32 == place, block_of(part, slot, crel), base)
                place += 1
        index = base * 32 + lane % 32
        top = []
        for yq in (0, 1):
            allow = index < len_ref[own_blocks[yq]]
            t = jnp.where(allow, s[yq * 128 : yq * 128 + 128, :], -jnp.inf)
            s_buf[16 + crel * 2 + group, yq * 128 : yq * 128 + 128, :] = t
            top.append(jnp.maximum(t[:, :128], t[:, 128:]))
        return jnp.concatenate(top, axis=0)

    def absorb(chunks):
        tops = [mem_scores(*c[1:]) if c[0] else seq_scores(*c[1:]) for c in chunks]
        top = functools.reduce(jnp.maximum, tops)
        old = m_scr[...]
        new = jnp.maximum(old, jnp.broadcast_to(jnp.max(top, axis=1, keepdims=True), old.shape))
        fade = jnp.exp2(old - new)
        total = l_scr[...] * fade
        accum = acc_scr[...] * fade
        for mem, crel, slot in chunks:
            j = 16 + crel * 2 + slot if mem else crel * 8 + slot
            values = mem_rows(crel, slot, MV0) if mem else both(g1, crel, slot, V0, 128)
            p = jnp.exp2(s_buf[j] - jnp.concatenate([new, new], axis=1))
            total = total + p[:, :128] + p[:, 128:]
            high = p.astype(BF16)
            low = (p - high.astype(F32)).astype(BF16)
            accum = accum + dot_nn(high, values) + dot_nn(low, values)
        m_scr[...] = new
        l_scr[...] = total
        acc_scr[...] = accum

    def take_sib(phase, *slots):
        for slot in slots:
            sib(phase, slot).wait_recv()

    absorb([(0, 0, 0)])
    advance(0, 0)
    absorb([(0, 0, 1), (0, 0, 2)])
    take_sib(0, 0)
    absorb([(0, 1, 0)])
    advance(0, 1)
    absorb([(0, 0, 3), (0, 0, 4)])
    take_sib(0, 1, 2)
    absorb([(0, 1, 1), (0, 1, 2)])
    advance(0, 2)
    y_do.wait_recv()
    ring_send(1, 0, 0)
    ring_send(1, 0, 1)
    go(sib(1, 0))
    absorb([(0, 0, 5), (0, 0, 6), (1, 0, 0)])
    take_sib(0, 3, 4)
    absorb([(0, 1, 3), (0, 1, 4)])
    advance(0, 3)
    absorb([(0, 0, 7), (1, 0, 1)])
    take_sib(0, 5, 6)
    absorb([(0, 1, 5), (0, 1, 6), (1, 1, 0)])
    take_sib(0, 7)
    absorb([(0, 1, 7), (1, 1, 1)])

    total = jnp.broadcast_to(jnp.sum(l_scr[...], axis=1, keepdims=True), (256, 128))
    lse = m_scr[...] + jnp.log2(total)
    attended = (acc_scr[...] / total).astype(BF16)
    o_scr[...] = attended
    y_o = go(remote(o_scr, on_scr, y_ss.at[7], y_rs.at[7], y_dev))
    do_mine = both(g2, 0, 0, D0, 128)
    delta = jnp.broadcast_to(
        jnp.sum(do_mine.astype(F32) * attended.astype(F32), axis=1, keepdims=True), (256, 128)
    )
    m_scr[...] = lse
    l_scr[...] = delta
    eye = lax.broadcasted_iota(jnp.int32, (128, 128), 0) == lax.broadcasted_iota(
        jnp.int32, (128, 128), 1
    )
    ld[0, 0] = jnp.zeros((8, 256), F32)
    for yq in (0, 1):
        rows = slice(yq * 128, yq * 128 + 128)
        ld[0, 0, 0:1, rows] = jnp.sum(jnp.where(eye, lse[rows, :], 0.0), axis=0, keepdims=True)
        ld[0, 0, 1:2, rows] = jnp.sum(jnp.where(eye, delta[rows, :], 0.0), axis=0, keepdims=True)

    def ld_copy(off):
        slot = SLOT_OF[(-off) % NZ]
        return remote(
            ld.at[0, 0], ld.at[0, slot], ld_ss.at[slot - 1], ld_rs.at[slot - 1], at(i, z_at(off), core)
        )

    for off in (4, 3, 5, 2, 6, 1, 7):
        go(ld_copy(off))
    advance(1, 0)

    y_o.wait_recv()
    att_scr[i] = o_scr[0:128, :]
    att_scr[1 - i] = on_scr[128:256, :]
    att_own = jnp.concatenate([att_scr[0], att_scr[1]], axis=1)
    width = w_hbm.shape[1] // heads_n

    def lo_copy(k):
        return remote(
            lo_send.at[k - 1],
            lo_recv.at[k - 1],
            lo_ss.at[k - 1],
            lo_rs.at[k - 1],
            {"head": lax.rem(head + k, heads_n)},
        )

    for k in list(range(1, heads_n)) + [0]:
        cols = pl.ds(pl.multiple_of(lax.rem(head + k, heads_n) * width, HD), width)
        part = dot_nn(att_own, w_buf[:, cols])
        if k:
            lo_send[k - 1] = part.astype(BF16)
            go(lo_copy(k))
        else:
            lo_own[...] = part
    advance(1, 1)

    att_scr2 = jnp.concatenate([on_scr[128:256, :], on_scr[0:128, :]], axis=0)
    pair = (o_scr[...], att_scr2)
    att_t = jnp.concatenate(
        [
            jnp.where(i == 0, pair[0].astype(F32), pair[1].astype(F32)).T,
            jnp.where(i == 0, pair[1].astype(F32), pair[0].astype(F32)).T,
        ],
        axis=0,
    ).astype(BF16)
    y_og.wait_recv()

    def gw_part(k, cc):
        col = (z_at(k) * 2 + cc) * HD
        grads_in = jnp.concatenate(
            [
                og_buf[:, pl.ds(pl.multiple_of(i * half + col, HD), HD)],
                ogx[:, pl.ds(pl.multiple_of(col, HD), HD)],
            ],
            axis=0,
        )
        return dot_nn(att_t, grads_in)

    for k in range(NZ):
        gs_send[k] = gw_part(k, 1 - core).astype(BF16)
    gw_sib = go(remote(gs_send, gs_recv, y_ss.at[8], y_rs.at[8], sib_dev))
    for k in range(NZ):
        gw_acc[k] = gw_part(k, core)
    advance(1, 2)

    def gw_copy(k):
        return remote(
            gw_send.at[k - 1],
            gw_recv.at[k - 1],
            gw_ss.at[k - 1],
            gw_rs.at[k - 1],
            at(i, z_at(k), core),
        )

    gw_sib.wait_recv()
    for k in (4, 3, 5, 2, 6, 1, 7):
        gw_send[k - 1] = (gw_acc[k] + gs_recv[k].astype(F32)).astype(BF16)
        go(gw_copy(k))
    gw_own = gw_acc[0] + gs_recv[0].astype(F32)
    gw_acc[0] = gw_own

    for off in range(1, NZ):
        ld_copy(off).wait_recv()
    ld_sib = go(remote(ld.at[0], ld.at[1], y_ss.at[9], y_rs.at[9], sib_dev))

    dq_scr[...] = jnp.zeros_like(dq_scr)

    def query_step(j, keys, values):
        p = jnp.exp2(s_buf[j] - jnp.concatenate([m_scr[...], m_scr[...]], axis=1))
        dp = dot_nt(do_mine, values)
        ds = (p * (dp - jnp.concatenate([l_scr[...], l_scr[...]], axis=1))).astype(BF16)
        dq_scr[...] += dot_nn(ds, keys)

    def query_loop(slot, carry):
        for crel in (0, 1):
            query_step(
                crel * 8 + slot, both(g1, crel, slot, K0, 128), both(g1, crel, slot, V0, 128)
            )
        return carry

    lax.fori_loop(0, NZ, query_loop, 0)
    for crel in (0, 1):
        for group in (0, 1):
            query_step(
                16 + crel * 2 + group, mem_rows(crel, group, MK0), mem_rows(crel, group, MV0)
            )
    finish = []

    def give(kind, out, value):
        grads[kind] = value.astype(BF16)
        copy = pltpu.make_async_copy(grads.at[kind, 0:128], out.at[:, own_cols], out_sem.at[kind])
        copy.start()
        finish.append(copy)
        return go(
            remote(
                grads.at[kind, 128:256],
                out.at[:, own_cols],
                y_ss.at[10 + kind],
                y_rs.at[10 + kind],
                y_dev,
            )
        )

    given = [give(0, gq_out, dq_scr[...] * scale)]
    advance(1, 3)
    take_sib(1, *range(NZ))
    ld_sib.wait_recv()

    k_mine = both(g1, 0, 0, K0, 128)
    v_mine = both(g1, 0, 0, V0, 128)
    dk_scr[...] = jnp.zeros_like(dk_scr)
    dv_scr[...] = jnp.zeros_like(dv_scr)

    def key_step(crel, slot):
        queries = both(g2, crel, slot, Q0, 128)
        grad_out = both(g2, crel, slot, D0, 128)
        lse_row = ld[crel, slot, 0:1, :]
        delta_row = ld[crel, slot, 1:2, :]
        s = dot_nt(k_mine, queries) * (scale * LOG2E)
        rows = []
        for yk in (0, 1):
            row = []
            for yq in (0, 1):
                bias = jnp.where(
                    mask_ref[block_of(yq, slot, crel), own_blocks[yk]] > 0, 0.0, -jnp.inf
                )
                cut = slice(yq * 128, yq * 128 + 128)
                row.append(
                    jnp.exp2(s[yk * 128 : yk * 128 + 128, cut] + (bias - lse_row[:, cut]))
                )
            rows.append(jnp.concatenate(row, axis=1))
        p = jnp.concatenate(rows, axis=0)
        dp = dot_nt(v_mine, grad_out)
        ds = (p * (dp - delta_row)).astype(BF16)
        dv_scr[...] += dot_nn(p.astype(BF16), grad_out)
        dk_scr[...] += dot_nn(ds, queries)

    for slot in range(NZ):
        for crel in (0, 1):
            key_step(crel, slot)
    given.append(give(1, gk_out, dk_scr[...] * scale))
    given.append(give(2, gv_out, dv_scr[...]))

    result = lo_own[...]
    for k in range(1, heads_n):
        lo_copy(k).wait_recv()
        result = result + lo_recv[k - 1].astype(F32)
    lo_stage[...] = result.astype(BF16)
    copy = pltpu.make_async_copy(lo_stage, lo_out, out_sem.at[3])
    copy.start()
    finish.append(copy)
    result = gw_acc[0]
    for k in range(1, NZ):
        gw_copy(k).wait_recv()
        result = result + gw_recv[k - 1].astype(F32)
    gw_stage[...] = result.astype(BF16)
    copy = pltpu.make_async_copy(gw_stage, gw_out, out_sem.at[4])
    copy.start()
    finish.append(copy)

    for copy in given:
        copy.wait_recv()
    for copy in finish:
        copy.wait()
    for copy in started:
        copy.wait_send()


def per_device(
    queries,
    key_states,
    value_states,
    memory_keys,
    memory_values,
    memory_length,
    block_mask,
    out_weight,
    out_grad,
    *,
    heads_n,
):
    rows, cols = queries.shape
    d_model = out_weight.shape[1]
    width = d_model // heads_n
    hbm = pl.BlockSpec(memory_space=pltpu.HBM)
    smem = pl.BlockSpec(memory_space=pltpu.SMEM)
    vm = pltpu.VMEM
    dma = pltpu.SemaphoreType.DMA
    grad_shape = jax.ShapeDtypeStruct((rows, cols), BF16)
    return pl.pallas_call(
        functools.partial(kernel, heads_n),
        out_shape=(
            jax.ShapeDtypeStruct((rows, width), BF16),
            jax.ShapeDtypeStruct((cols, HD), BF16),
            grad_shape,
            grad_shape,
            grad_shape,
        ),
        in_specs=[smem, smem] + [hbm] * 7,
        out_specs=(hbm,) * 5,
        scratch_shapes=[
            vm((2, NZ, 2, ROWS1, HD), BF16),
            vm((2, NZ, 2, ROWS2, HD), BF16),
            vm((20, 256, 256), F32),
            vm((cols, d_model), BF16),
            vm((rows, d_model), BF16),
            vm((rows, d_model // 2), BF16),
            vm((2, rows, HD), BF16),
            vm((256, HD), BF16),
            vm((256, HD), BF16),
            vm((2, rows, HD), BF16),
            vm((2, NZ, 8, 256), F32),
            vm((rows, width), F32),
            vm((max(heads_n - 1, 1), rows, width), BF16),
            vm((max(heads_n - 1, 1), rows, width), BF16),
            vm((NZ, 256, HD), BF16),
            vm((NZ, 256, HD), BF16),
            vm((NZ, 256, HD), F32),
            vm((NZ - 1, 256, HD), BF16),
            vm((NZ - 1, 256, HD), BF16),
            vm((256, HD), F32),
            vm((256, HD), F32),
            vm((256, HD), F32),
            vm((256, HD), F32),
            vm((256, HD), F32),
            vm((256, HD), F32),
            vm((3, 256, HD), BF16),
            vm((rows, width), BF16),
            vm((cols, HD), BF16),
            dma((7,)),
            dma((2, 2, 4, 2)),
            dma((2, 2, 4, 2)),
            dma((2, NZ)),
            dma((2, NZ)),
            dma((13,)),
            dma((13,)),
            dma((NZ - 1,)),
            dma((NZ - 1,)),
            dma((max(heads_n - 1, 1),)),
            dma((max(heads_n - 1, 1),)),
            dma((NZ - 1,)),
            dma((NZ - 1,)),
            dma((5,)),
        ],
        compiler_params=pltpu.CompilerParams(
            collective_id=0, has_side_effects=True, vmem_limit_bytes=48 * 1024 * 1024
        ),
        name="attention",
    )(
        memory_length,
        block_mask,
        queries,
        key_states,
        value_states,
        memory_keys,
        memory_values,
        out_weight,
        out_grad,
    )


def solution(mesh):
    in_specs = (
        P("ctx", "head"),
        P("ctx", "head"),
        P("ctx", "head"),
        P("ctx", "head"),
        P("ctx", "head"),
        P(),
        P(),
        P("head", None),
        P("ctx", None),
    )
    out_specs = (
        P("ctx", "head"),
        P("head", "ctx"),
        P("ctx", "head"),
        P("ctx", "head"),
        P("ctx", "head"),
    )
    return jax.shard_map(
        functools.partial(per_device, heads_n=mesh.shape["head"]),
        mesh=mesh,
        in_specs=in_specs,
        out_specs=out_specs,
        check_vma=False,
    )
```

time: 612 us -> 74.2 us (0.12)
  the two profiles are of different devices: /device:TPU:4 before, /device:TPU:1 now
where the time goes in v1:
time: 74.2 us; the launch traced here: 73.7 us
  Pallas kernels  61.7 us (83%)
  local copies, waits for them, and re-layouts  11.3 us (15%)
    pallas_call x1, Pallas kernels, per_device(): pl.pallas_call(functools.partial(kernel, heads_n), out_shape=(jax.ShapeDt...  61.7 us
    unnamed x23, local copies, waits for them, and re-layouts  11.3 us

profile of v1, /device:TPU:1, one launch (start us, length us, event | category | flops | bytes accessed | tf_op | source)
XLA Modules:
  0.0 73.7 jit_solution(13642285031887702074)
XLA Ops:
  0.6 0.0 copy-start
  0.6 1.6 %copy-done = bf16[256,4096]{1,0:T(8,128)(2,1)S(1)} copy-done((bf16[256,4096]{1,0:T(8,128)(2,1)S(1)}, bf16[256,4096]{1,0:T(8,128)(2,1)}, u32[]{:S(2)}) %copy-start) | copy-done | bytes 2097176
  2.2 0.0 copy-start.1
  2.2 1.2 %copy-done.1 = bf16[128,4096]{1,0:T(8,128)(2,1)S(1)} copy-done((bf16[128,4096]{1,0:T(8,128)(2,1)S(1)}, bf16[128,4096]{1,0:T(8,128)(2,1)}, u32[]{:S(2)}) %copy-start.1) | copy-done | bytes 1048600
  3.5 0.0 copy-start.2
  3.5 0.8 %copy-done.2 = bf16[128,256]{1,0:T(8,128)(2,1)S(1)} copy-done((bf16[128,256]{1,0:T(8,128)(2,1)S(1)}, bf16[128,256]{1,0:T(8,128)(2,1)}, u32[]{:S(2)}) %copy-start.2) | copy-done | bytes 65560
  4.3 0.0 copy-start.3
  4.3 0.8 %copy-done.3 = bf16[128,256]{1,0:T(8,128)(2,1)S(1)} copy-done((bf16[128,256]{1,0:T(8,128)(2,1)S(1)}, bf16[128,256]{1,0:T(8,128)(2,1)}, u32[]{:S(2)}) %copy-start.3) | copy-done | bytes 65560
  5.1 0.0 copy-start.4
  5.1 0.8 %copy-done.4 = bf16[128,256]{1,0:T(8,128)(2,1)S(1)} copy-done((bf16[128,256]{1,0:T(8,128)(2,1)S(1)}, bf16[128,256]{1,0:T(8,128)(2,1)}, u32[]{:S(2)}) %copy-start.4) | copy-done | bytes 65560
  6.0 0.0 copy-start.5
  6.0 0.7 copy-done.5
  6.7 0.0 copy-start.6
  6.7 0.7 copy-done.6
  7.4 0.0 copy-start.7
  7.4 0.7 copy-done.7
  8.1 0.0 copy-start.8
  8.1 0.7 copy-done.8
  8.8 61.7 %attention.1 = (bf16[128,512]{1,0:T(8,128)(2,1)S(1)}, bf16[256,128]{1,0:T(8,128)(2,1)S(1)}, bf16[128,256]{1,0:T(8,128)(2,1)S(1)}, bf16[128,256]{1,0:T(8,128)(2,1)S(1)}, bf16[128,256]{1,0:T(8,128)(2,1)S(1)}) custom-call(s32[32]{0:T(128)S(1)} %copy-done.8, s32[32,32]{1,0:T(8,128)S(1)} %copy-done.5, bf16[128,256]{1,0:T(8,128)(2,1)S(1)} %copy-done.2, ...), custom_call_target="tpu_custom_call" | custom-call | tf_op jit(solution)/shard_map/attention/pallas_call | solution.py:565
  70.5 0.7 copy.19
  71.2 0.6 copy.20
  71.8 0.6 copy.21
  72.4 0.6 copy.22
  73.1 0.6 copy.23
Async XLA Ops:
  0.6 1.6 %copy-start = (bf16[256,4096]{1,0:T(8,128)(2,1)S(1)}, bf16[256,4096]{1,0:T(8,128)(2,1)}, u32[]{:S(2)}) copy-start(bf16[256,4096]{1,0:T(8,128)(2,1)} %w_hbm.1) | copy-start | bytes 6291460
  2.2 1.2 %copy-start.1 = (bf16[128,4096]{1,0:T(8,128)(2,1)S(1)}, bf16[128,4096]{1,0:T(8,128)(2,1)}, u32[]{:S(2)}) copy-start(bf16[128,4096]{1,0:T(8,128)(2,1)} %og_hbm.1) | copy-start | bytes 3145732
  3.5 0.8 %copy-start.2 = (bf16[128,256]{1,0:T(8,128)(2,1)S(1)}, bf16[128,256]{1,0:T(8,128)(2,1)}, u32[]{:S(2)}) copy-start(bf16[128,256]{1,0:T(8,128)(2,1)} %q_hbm.1) | copy-start | bytes 196612
  4.3 0.8 %copy-start.3 = (bf16[128,256]{1,0:T(8,128)(2,1)S(1)}, bf16[128,256]{1,0:T(8,128)(2,1)}, u32[]{:S(2)}) copy-start(bf16[128,256]{1,0:T(8,128)(2,1)} %k_hbm.1) | copy-start | bytes 196612
  5.1 0.8 %copy-start.4 = (bf16[128,256]{1,0:T(8,128)(2,1)S(1)}, bf16[128,256]{1,0:T(8,128)(2,1)}, u32[]{:S(2)}) copy-start(bf16[128,256]{1,0:T(8,128)(2,1)} %v_hbm.1) | copy-start | bytes 196612
  6.0 0.7 copy-start.5
  6.7 0.7 copy-start.6
  7.4 0.7 copy-start.7
  8.1 0.7 copy-start.8

commit v2 on v1

--- a/solution.py
+++ b/solution.py
@@ -11,6 +11,9 @@
 HD = 128
 BLK = 128
 NZ = 8
+NX = 4
+LAG = 3
+GW_ORDER = (4, 3, 5, 2, 6, 1, 7, 0)
 F32 = jnp.float32
 BF16 = jnp.bfloat16
 MESH = pl.DeviceIdType.MESH
@@ -89,6 +92,7 @@
     gw_ss,
     gw_rs,
     out_sem,
+    hello,
 ):
     ctx = lax.axis_index("ctx")
     head = lax.axis_index("head")
@@ -139,11 +143,21 @@
     local_w.start()
 
     barrier = pltpu.get_barrier_semaphore()
-    peers = [y_dev, sib_dev]
-    peers += [at(i, z_at(off), core) for off in range(1, NZ)]
-    peers += [{"head": lax.rem(head + k, heads_n)} for k in range(1, heads_n)]
+    x = lax.rem(head, NX)
+    row = head - x
+    x_next = {"head": row + lax.rem(x + 1, NX)}
+    x_last = {"head": row + lax.rem(x + NX - 1, NX)}
+    row_dev = {"head": lax.rem(head + NX, heads_n)}
+    peers = [y_dev, sib_dev, at(i, z_at(1), core), at(i, z_at(-1), core), x_next, x_last, row_dev]
     for dev in peers:
         pl.semaphore_signal(barrier, inc=1, device_id=dev, device_id_type=MESH)
+
+    local_og.wait()
+    local_w.wait()
+    grad_att = dot_nt(og_buf[...], w_buf[...]).astype(BF16)
+    do_scr[0] = grad_att[:, :HD]
+    do_scr[1] = grad_att[:, HD:]
+    g2[0, 0, 0, D0 : D0 + 128, :] = do_scr[i]
     pl.semaphore_wait(barrier, len(peers))
 
     far = g1.at[0, 0, 1]
@@ -159,6 +173,9 @@
     for copy in y_first:
         go(copy)
     go(y_q)
+    y_do = go(
+        remote(do_scr.at[1 - i], g2.at[0, 0, 1, D0 : D0 + 128], y_ss.at[5], y_rs.at[5], y_dev)
+    )
 
     def ring(phase, way, step, part):
         src = 0 if step == 0 else 2 * step - 1 + way
@@ -183,12 +200,30 @@
             buf.at[0, slot], buf.at[1, slot], sib_ss.at[phase, slot], sib_rs.at[phase, slot], sib_dev
         )
 
+    def follow(step):
+        if step == LAG - 1:
+            if LAG == 0:
+                local_q.wait()
+            ring_send(1, 0, 0)
+            if LAG == 0:
+                y_q.wait_recv()
+            y_do.wait_recv()
+            ring_send(1, 0, 1)
+            go(sib(1, 0))
+        elif step >= LAG:
+            advance(1, step - LAG)
+
+    def take(phase, step, part):
+        for way in (0, 1):
+            ring(phase, way, step, part).wait_recv()
+            if step < 2 or part == way:
+                go(ring(phase, way, step + 1, part))
+
     def advance(phase, step):
         if step < 3:
             for part in (0, 1):
-                for way in (0, 1):
-                    ring(phase, way, step, part).wait_recv()
-                ring_send(phase, step + 1, part)
+                if (phase, step, part) != (0, 0, 0):
+                    take(phase, step, part)
             go(sib(phase, 2 * step + 1))
             go(sib(phase, 2 * step + 2))
         else:
@@ -199,20 +234,13 @@
     for copy in local1:
         copy.wait()
     ring_send(0, 0, 0)
+    pl.semaphore_signal(hello.at[0], inc=1, device_id=x_next, device_id_type=MESH)
+
+    take(0, 0, 0)
     for copy in y_first:
         copy.wait_recv()
     ring_send(0, 0, 1)
     go(sib(0, 0))
-
-    local_og.wait()
-    local_w.wait()
-    grad_att = dot_nt(og_buf[...], w_buf[...]).astype(BF16)
-    do_scr[0] = grad_att[:, :HD]
-    do_scr[1] = grad_att[:, HD:]
-    g2[0, 0, 0, D0 : D0 + 128, :] = do_scr[i]
-    y_do = go(
-        remote(do_scr.at[1 - i], g2.at[0, 0, 1, D0 : D0 + 128], y_ss.at[5], y_rs.at[5], y_dev)
-    )
     half = og_hbm.shape[1] // 2
     y_og = go(
         remote(
@@ -223,8 +251,10 @@
             y_dev,
         )
     )
-    local_q.wait()
-    y_q.wait_recv()
+    follow(-1)
+    if LAG > 0:
+        local_q.wait()
+        y_q.wait_recv()
 
     def block_of(part, slot, crel):
         ii = i if part == 0 else 1 - i
@@ -306,28 +336,34 @@
         l_scr[...] = total
         acc_scr[...] = accum
 
+    def late(step):
+        if step > 3 - LAG:
+            advance(1, step)
+
     def take_sib(phase, *slots):
         for slot in slots:
             sib(phase, slot).wait_recv()
 
     absorb([(0, 0, 0)])
+    pl.semaphore_wait(hello.at[0], 1)
+    pl.semaphore_signal(hello.at[1], inc=1, device_id=row_dev, device_id_type=MESH)
     advance(0, 0)
+    follow(0)
     absorb([(0, 0, 1), (0, 0, 2)])
     take_sib(0, 0)
     absorb([(0, 1, 0)])
     advance(0, 1)
+    follow(1)
     absorb([(0, 0, 3), (0, 0, 4)])
     take_sib(0, 1, 2)
     absorb([(0, 1, 1), (0, 1, 2)])
     advance(0, 2)
-    y_do.wait_recv()
-    ring_send(1, 0, 0)
-    ring_send(1, 0, 1)
-    go(sib(1, 0))
+    follow(2)
     absorb([(0, 0, 5), (0, 0, 6), (1, 0, 0)])
     take_sib(0, 3, 4)
     absorb([(0, 1, 3), (0, 1, 4)])
     advance(0, 3)
+    follow(3)
     absorb([(0, 0, 7), (1, 0, 1)])
     take_sib(0, 5, 6)
     absorb([(0, 1, 5), (0, 1, 6), (1, 1, 0)])
@@ -362,33 +398,28 @@
 
     for off in (4, 3, 5, 2, 6, 1, 7):
         go(ld_copy(off))
-    advance(1, 0)
+    late(0)
+
+    dq_scr[...] = jnp.zeros_like(dq_scr)
+
+    def query_step(j, keys, values):
+        p = jnp.exp2(s_buf[j] - jnp.concatenate([m_scr[...], m_scr[...]], axis=1))
+        dp = dot_nt(do_mine, values)
+        ds = (p * (dp - jnp.concatenate([l_scr[...], l_scr[...]], axis=1))).astype(BF16)
+        dq_scr[...] += dot_nn(ds, keys)
+
+    def query_loop(slot, carry):
+        for crel in (0, 1):
+            query_step(
+                crel * 8 + slot, both(g1, crel, slot, K0, 128), both(g1, crel, slot, V0, 128)
+            )
+        return carry
+
+    lax.fori_loop(0, 3, query_loop, 0)
+    late(1)
+    lax.fori_loop(3, 5, query_loop, 0)
 
     y_o.wait_recv()
-    att_scr[i] = o_scr[0:128, :]
-    att_scr[1 - i] = on_scr[128:256, :]
-    att_own = jnp.concatenate([att_scr[0], att_scr[1]], axis=1)
-    width = w_hbm.shape[1] // heads_n
-
-    def lo_copy(k):
-        return remote(
-            lo_send.at[k - 1],
-            lo_recv.at[k - 1],
-            lo_ss.at[k - 1],
-            lo_rs.at[k - 1],
-            {"head": lax.rem(head + k, heads_n)},
-        )
-
-    for k in list(range(1, heads_n)) + [0]:
-        cols = pl.ds(pl.multiple_of(lax.rem(head + k, heads_n) * width, HD), width)
-        part = dot_nn(att_own, w_buf[:, cols])
-        if k:
-            lo_send[k - 1] = part.astype(BF16)
-            go(lo_copy(k))
-        else:
-            lo_own[...] = part
-    advance(1, 1)
-
     att_scr2 = jnp.concatenate([on_scr[128:256, :], on_scr[0:128, :]], axis=0)
     pair = (o_scr[...], att_scr2)
     att_t = jnp.concatenate(
@@ -411,12 +442,18 @@
         )
         return dot_nn(att_t, grads_in)
 
-    for k in range(NZ):
-        gs_send[k] = gw_part(k, 1 - core).astype(BF16)
-    gw_sib = go(remote(gs_send, gs_recv, y_ss.at[8], y_rs.at[8], sib_dev))
-    for k in range(NZ):
-        gw_acc[k] = gw_part(k, core)
-    advance(1, 2)
+    gw_sib = []
+    for place, k in enumerate(GW_ORDER):
+        gs_send[place] = gw_part(k, 1 - core).astype(BF16)
+        if place % 4 == 3:
+            cut = slice(place - 3, place + 1)
+            n = 8 if place == 3 else 13
+            gw_sib.append(
+                go(remote(gs_send.at[cut], gs_recv.at[cut], y_ss.at[n], y_rs.at[n], sib_dev))
+            )
+    for place, k in enumerate(GW_ORDER):
+        gw_acc[place] = gw_part(k, core)
+    late(2)
 
     def gw_copy(k):
         return remote(
@@ -427,33 +464,44 @@
             at(i, z_at(k), core),
         )
 
-    gw_sib.wait_recv()
-    for k in (4, 3, 5, 2, 6, 1, 7):
-        gw_send[k - 1] = (gw_acc[k] + gs_recv[k].astype(F32)).astype(BF16)
-        go(gw_copy(k))
-    gw_own = gw_acc[0] + gs_recv[0].astype(F32)
-    gw_acc[0] = gw_own
+    for place, k in enumerate(GW_ORDER):
+        if place % 4 == 0:
+            gw_sib[place // 4].wait_recv()
+        block = gw_acc[place] + gs_recv[place].astype(F32)
+        if k:
+            gw_send[k - 1] = block.astype(BF16)
+            go(gw_copy(k))
+        else:
+            gw_acc[0] = block
+
+    pl.semaphore_wait(hello.at[1], 1)
+    att_scr[i] = o_scr[0:128, :]
+    att_scr[1 - i] = on_scr[128:256, :]
+    att_own = jnp.concatenate([att_scr[0], att_scr[1]], axis=1)
+    width = w_hbm.shape[1] // heads_n
+
+    def lo_copy(k):
+        return remote(
+            lo_send.at[k - 1],
+            lo_recv.at[k - 1],
+            lo_ss.at[k - 1],
+            lo_rs.at[k - 1],
+            {"head": lax.rem(head + k, heads_n)},
+        )
+
+    for k in list(range(1, heads_n)) + [0]:
+        cols = pl.ds(pl.multiple_of(lax.rem(head + k, heads_n) * width, HD), width)
+        part = dot_nn(att_own, w_buf[:, cols])
+        if k:
+            lo_send[k - 1] = part.astype(BF16)
+            go(lo_copy(k))
+        else:
+            lo_own[...] = part
 
     for off in range(1, NZ):
         ld_copy(off).wait_recv()
     ld_sib = go(remote(ld.at[0], ld.at[1], y_ss.at[9], y_rs.at[9], sib_dev))
-
-    dq_scr[...] = jnp.zeros_like(dq_scr)
-
-    def query_step(j, keys, values):
-        p = jnp.exp2(s_buf[j] - jnp.concatenate([m_scr[...], m_scr[...]], axis=1))
-        dp = dot_nt(do_mine, values)
-        ds = (p * (dp - jnp.concatenate([l_scr[...], l_scr[...]], axis=1))).astype(BF16)
-        dq_scr[...] += dot_nn(ds, keys)
-
-    def query_loop(slot, carry):
-        for crel in (0, 1):
-            query_step(
-                crel * 8 + slot, both(g1, crel, slot, K0, 128), both(g1, crel, slot, V0, 128)
-            )
-        return carry
-
-    lax.fori_loop(0, NZ, query_loop, 0)
+    lax.fori_loop(5, NZ, query_loop, 0)
     for crel in (0, 1):
         for group in (0, 1):
             query_step(
@@ -477,7 +525,7 @@
         )
 
     given = [give(0, gq_out, dq_scr[...] * scale)]
-    advance(1, 3)
+    late(3)
     take_sib(1, *range(NZ))
     ld_sib.wait_recv()
 
@@ -541,6 +589,19 @@
         copy.wait_send()
 
 
+def hand_out(*refs):
+    ins, outs, held, sems = refs[:5], refs[5:10], refs[10:15], refs[15]
+    reads = [pltpu.make_async_copy(ins[n], held[n], sems.at[0, n]) for n in range(5)]
+    writes = [pltpu.make_async_copy(held[n], outs[n], sems.at[1, n]) for n in range(5)]
+    for copy in reads:
+        copy.start()
+    for n in range(5):
+        reads[n].wait()
+        writes[n].start()
+    for copy in writes:
+        copy.wait()
+
+
 def per_device(
     queries,
     key_states,
@@ -562,7 +623,7 @@
     vm = pltpu.VMEM
     dma = pltpu.SemaphoreType.DMA
     grad_shape = jax.ShapeDtypeStruct((rows, cols), BF16)
-    return pl.pallas_call(
+    results = pl.pallas_call(
         functools.partial(kernel, heads_n),
         out_shape=(
             jax.ShapeDtypeStruct((rows, width), BF16),
@@ -607,8 +668,8 @@
             dma((2, 2, 4, 2)),
             dma((2, NZ)),
             dma((2, NZ)),
-            dma((13,)),
-            dma((13,)),
+            dma((14,)),
+            dma((14,)),
             dma((NZ - 1,)),
             dma((NZ - 1,)),
             dma((max(heads_n - 1, 1),)),
@@ -616,9 +677,10 @@
             dma((NZ - 1,)),
             dma((NZ - 1,)),
             dma((5,)),
+            pltpu.SemaphoreType.REGULAR((2,)),
         ],
         compiler_params=pltpu.CompilerParams(
-            collective_id=0, has_side_effects=True, vmem_limit_bytes=48 * 1024 * 1024
+            collective_id=0, has_side_effects=True, vmem_limit_bytes=56 * 1024 * 1024
         ),
         name="attention",
     )(
@@ -632,6 +694,14 @@
         out_weight,
         out_grad,
     )
+    return pl.pallas_call(
+        hand_out,
+        out_shape=tuple(jax.ShapeDtypeStruct(r.shape, r.dtype) for r in results),
+        in_specs=[hbm] * 5,
+        out_specs=(hbm,) * 5,
+        scratch_shapes=[vm(r.shape, r.dtype) for r in results] + [dma((2, 5))],
+        name="results",
+    )(*results)
 
 
 def solution(mesh):

time: 74.2 us -> 61.9 us (0.83)
  the two profiles are of different devices: /device:TPU:1 before, /device:TPU:4 now
where the time goes in v2:
time: 61.9 us; the launch traced here: 61.7 us
  Pallas kernels  60.9 us (98%)
  between operations  0.8 us (1%)
    pallas_call x1, Pallas kernels, per_device(): pl.pallas_call(functools.partial(kernel, heads_n), out_shape=(jax.ShapeDt...  59.2 us
    pallas_call x1, Pallas kernels, per_device(): pl.pallas_call(hand_out, out_shape=tuple((jax.ShapeDtypeStruct(r.shape, r...  1.73 us

profile of v2, /device:TPU:4, one launch (start us, length us, event | category | flops | bytes accessed | tf_op | source)
XLA Modules:
  0.0 61.7 jit_solution(13948108554902932792)
XLA Ops:
  0.6 59.2 %attention.1 = (bf16[128,512]{1,0:T(8,128)(2,1)}, bf16[256,128]{1,0:T(8,128)(2,1)}, bf16[128,256]{1,0:T(8,128)(2,1)}, bf16[128,256]{1,0:T(8,128)(2,1)}, bf16[128,256]{1,0:T(8,128)(2,1)}) custom-call(s32[32]{0:T(128)} %len_ref.1, s32[32,32]{1,0:T(8,128)} %mask_ref.1, bf16[128,256]{1,0:T(8,128)(2,1)} %q_hbm.1, bf16[128,256]{1,0:T(8,128)(2,1)} %k_hbm.1, ...), custom_call_target="tpu_custom_call" | custom-call | tf_op jit(solution)/shard_map/attention/pallas_call | solution.py:626
  59.8 1.7 %results.1 = (bf16[128,512]{1,0:T(8,128)(2,1)}, bf16[256,128]{1,0:T(8,128)(2,1)}, bf16[128,256]{1,0:T(8,128)(2,1)}, bf16[128,256]{1,0:T(8,128)(2,1)}, bf16[128,256]{1,0:T(8,128)(2,1)}) custom-call(bf16[128,512]{1,0:T(8,128)(2,1)} %get-tuple-element.10.refs_0_, bf16[256,128]{1,0:T(8,128)(2,1)} %get-tuple-element.11.refs_1_, ...), custom_call_target="tpu_custom_call" | custom-call | tf_op jit(solution)/shard_map/results/pallas_call | solution.py:697

commit v3 on v2

--- a/solution.py
+++ b/solution.py
@@ -453,6 +453,29 @@
             )
     for place, k in enumerate(GW_ORDER):
         gw_acc[place] = gw_part(k, core)
+    pl.semaphore_wait(hello.at[1], 1)
+    att_scr[i] = o_scr[0:128, :]
+    att_scr[1 - i] = on_scr[128:256, :]
+    att_own = jnp.concatenate([att_scr[0], att_scr[1]], axis=1)
+    width = w_hbm.shape[1] // heads_n
+
+    def lo_copy(k):
+        return remote(
+            lo_send.at[k - 1],
+            lo_recv.at[k - 1],
+            lo_ss.at[k - 1],
+            lo_rs.at[k - 1],
+            {"head": lax.rem(head + k, heads_n)},
+        )
+
+    for k in list(range(1, heads_n)) + [0]:
+        cols = pl.ds(pl.multiple_of(lax.rem(head + k, heads_n) * width, HD), width)
+        part = dot_nn(att_own, w_buf[:, cols])
+        if k:
+            lo_send[k - 1] = part.astype(BF16)
+            go(lo_copy(k))
+        else:
+            lo_own[...] = part
     late(2)
 
     def gw_copy(k):
@@ -473,30 +496,6 @@
             go(gw_copy(k))
         else:
             gw_acc[0] = block
-
-    pl.semaphore_wait(hello.at[1], 1)
-    att_scr[i] = o_scr[0:128, :]
-    att_scr[1 - i] = on_scr[128:256, :]
-    att_own = jnp.concatenate([att_scr[0], att_scr[1]], axis=1)
-    width = w_hbm.shape[1] // heads_n
-
-    def lo_copy(k):
-        return remote(
-            lo_send.at[k - 1],
-            lo_recv.at[k - 1],
-            lo_ss.at[k - 1],
-            lo_rs.at[k - 1],
-            {"head": lax.rem(head + k, heads_n)},
-        )
-
-    for k in list(range(1, heads_n)) + [0]:
-        cols = pl.ds(pl.multiple_of(lax.rem(head + k, heads_n) * width, HD), width)
-        part = dot_nn(att_own, w_buf[:, cols])
-        if k:
-            lo_send[k - 1] = part.astype(BF16)
-            go(lo_copy(k))
-        else:
-            lo_own[...] = part
 
     for off in range(1, NZ):
         ld_copy(off).wait_recv()
@@ -525,9 +524,8 @@
         )
 
     given = [give(0, gq_out, dq_scr[...] * scale)]
-    late(3)
-    take_sib(1, *range(NZ))
     ld_sib.wait_recv()
+    take_sib(1, *range(5))
 
     k_mine = both(g1, 0, 0, K0, 128)
     v_mine = both(g1, 0, 0, V0, 128)
@@ -558,9 +556,17 @@
         dv_scr[...] += dot_nn(p.astype(BF16), grad_out)
         dk_scr[...] += dot_nn(ds, queries)
 
-    for slot in range(NZ):
-        for crel in (0, 1):
-            key_step(crel, slot)
+    def key_steps(*slots):
+        for slot in slots:
+            for crel in (0, 1):
+                key_step(crel, slot)
+
+    key_steps(0, 1, 2, 3, 4)
+    late(3)
+    take_sib(1, 5, 6)
+    key_steps(5, 6)
+    take_sib(1, 7)
+    key_steps(7)
     given.append(give(1, gk_out, dk_scr[...] * scale))
     given.append(give(2, gv_out, dv_scr[...]))
 

time: 61.9 us -> 59.3 us (0.958)
  Pallas kernels: 60.9 us -> 58.2 us
    pallas_call x1, Pallas kernels: 59.2 us -> 56.5 us  [per_device(): pl.pallas_call(functools.partial(kernel, heads_n), out_shape=(jax.ShapeDt...]
where the time goes in v3:
time: 59.3 us; the launch traced here: 59.1 us
  Pallas kernels  58.2 us (98%)
  between operations  0.8 us (1%)
    pallas_call x1, Pallas kernels, per_device(): pl.pallas_call(functools.partial(kernel, heads_n), out_shape=(jax.ShapeDt...  56.5 us
    pallas_call x1, Pallas kernels, per_device(): pl.pallas_call(hand_out, out_shape=tuple((jax.ShapeDtypeStruct(r.shape, r...  1.73 us

profile of v3, /device:TPU:4, one launch (start us, length us, event | category | flops | bytes accessed | tf_op | source)
XLA Modules:
  0.0 59.1 jit_solution(2801653866475885040)
XLA Ops:
  0.6 56.5 %attention.1 = (bf16[128,512]{1,0:T(8,128)(2,1)}, bf16[256,128]{1,0:T(8,128)(2,1)}, bf16[128,256]{1,0:T(8,128)(2,1)}, bf16[128,256]{1,0:T(8,128)(2,1)}, bf16[128,256]{1,0:T(8,128)(2,1)}) custom-call(s32[32]{0:T(128)} %len_ref.1, s32[32,32]{1,0:T(8,128)} %mask_ref.1, bf16[128,256]{1,0:T(8,128)(2,1)} %q_hbm.1, bf16[128,256]{1,0:T(8,128)(2,1)} %k_hbm.1, ...), custom_call_target="tpu_custom_call" | custom-call | tf_op jit(solution)/shard_map/attention/pallas_call | solution.py:632
  57.2 1.7 %results.1 = (bf16[128,512]{1,0:T(8,128)(2,1)}, bf16[256,128]{1,0:T(8,128)(2,1)}, bf16[128,256]{1,0:T(8,128)(2,1)}, bf16[128,256]{1,0:T(8,128)(2,1)}, bf16[128,256]{1,0:T(8,128)(2,1)}) custom-call(bf16[128,512]{1,0:T(8,128)(2,1)} %get-tuple-element.10.refs_0_, bf16[256,128]{1,0:T(8,128)(2,1)} %get-tuple-element.11.refs_1_, ...), custom_call_target="tpu_custom_call" | custom-call | tf_op jit(solution)/shard_map/results/pallas_call | solution.py:703

commit v4 on v3

--- a/solution.py
+++ b/solution.py
@@ -152,12 +152,6 @@
     for dev in peers:
         pl.semaphore_signal(barrier, inc=1, device_id=dev, device_id_type=MESH)
 
-    local_og.wait()
-    local_w.wait()
-    grad_att = dot_nt(og_buf[...], w_buf[...]).astype(BF16)
-    do_scr[0] = grad_att[:, :HD]
-    do_scr[1] = grad_att[:, HD:]
-    g2[0, 0, 0, D0 : D0 + 128, :] = do_scr[i]
     pl.semaphore_wait(barrier, len(peers))
 
     far = g1.at[0, 0, 1]
@@ -169,12 +163,6 @@
     ]
     y_q = remote(
         q_hbm.at[:, other_cols], g2.at[0, 0, 1, Q0 : Q0 + 128], y_ss.at[4], y_rs.at[4], y_dev
-    )
-    for copy in y_first:
-        go(copy)
-    go(y_q)
-    y_do = go(
-        remote(do_scr.at[1 - i], g2.at[0, 0, 1, D0 : D0 + 128], y_ss.at[5], y_rs.at[5], y_dev)
     )
 
     def ring(phase, way, step, part):
@@ -201,7 +189,7 @@
         )
 
     def follow(step):
-        if step == LAG - 1:
+        if step == 1:
             if LAG == 0:
                 local_q.wait()
             ring_send(1, 0, 0)
@@ -210,7 +198,7 @@
             y_do.wait_recv()
             ring_send(1, 0, 1)
             go(sib(1, 0))
-        elif step >= LAG:
+        if step >= LAG:
             advance(1, step - LAG)
 
     def take(phase, step, part):
@@ -234,8 +222,20 @@
     for copy in local1:
         copy.wait()
     ring_send(0, 0, 0)
+    for copy in y_first:
+        go(copy)
+    go(y_q)
     pl.semaphore_signal(hello.at[0], inc=1, device_id=x_next, device_id_type=MESH)
 
+    local_og.wait()
+    local_w.wait()
+    grad_att = dot_nt(og_buf[...], w_buf[...]).astype(BF16)
+    do_scr[0] = grad_att[:, :HD]
+    do_scr[1] = grad_att[:, HD:]
+    g2[0, 0, 0, D0 : D0 + 128, :] = do_scr[i]
+    y_do = go(
+        remote(do_scr.at[1 - i], g2.at[0, 0, 1, D0 : D0 + 128], y_ss.at[5], y_rs.at[5], y_dev)
+    )
     take(0, 0, 0)
     for copy in y_first:
         copy.wait_recv()
@@ -415,9 +415,9 @@
             )
         return carry
 
-    lax.fori_loop(0, 3, query_loop, 0)
+    lax.fori_loop(0, 2, query_loop, 0)
     late(1)
-    lax.fori_loop(3, 5, query_loop, 0)
+    lax.fori_loop(2, 4, query_loop, 0)
 
     y_o.wait_recv()
     att_scr2 = jnp.concatenate([on_scr[128:256, :], on_scr[0:128, :]], axis=0)
@@ -500,7 +500,7 @@
     for off in range(1, NZ):
         ld_copy(off).wait_recv()
     ld_sib = go(remote(ld.at[0], ld.at[1], y_ss.at[9], y_rs.at[9], sib_dev))
-    lax.fori_loop(5, NZ, query_loop, 0)
+    lax.fori_loop(4, NZ, query_loop, 0)
     for crel in (0, 1):
         for group in (0, 1):
             query_step(

time: 59.3 us -> 57.8 us (0.975)
  Pallas kernels: 58.2 us -> 56.9 us
    pallas_call x1, Pallas kernels: 56.5 us -> 55.1 us  [per_device(): pl.pallas_call(functools.partial(kernel, heads_n), out_shape=(jax.ShapeDt...]
where the time goes in v4:
time: 57.8 us; the launch traced here: 57.7 us
  Pallas kernels  56.9 us (98%)
  between operations  0.8 us (1%)
    pallas_call x1, Pallas kernels, per_device(): pl.pallas_call(functools.partial(kernel, heads_n), out_shape=(jax.ShapeDt...  55.1 us
    pallas_call x1, Pallas kernels, per_device(): pl.pallas_call(hand_out, out_shape=tuple((jax.ShapeDtypeStruct(r.shape, r...  1.73 us

profile of v4, /device:TPU:4, one launch (start us, length us, event | category | flops | bytes accessed | tf_op | source)
XLA Modules:
  0.0 57.7 jit_solution(4515981571451838065)
XLA Ops:
  0.6 55.1 %attention.1 = (bf16[128,512]{1,0:T(8,128)(2,1)}, bf16[256,128]{1,0:T(8,128)(2,1)}, bf16[128,256]{1,0:T(8,128)(2,1)}, bf16[128,256]{1,0:T(8,128)(2,1)}, bf16[128,256]{1,0:T(8,128)(2,1)}) custom-call(s32[32]{0:T(128)} %len_ref.1, s32[32,32]{1,0:T(8,128)} %mask_ref.1, bf16[128,256]{1,0:T(8,128)(2,1)} %q_hbm.1, bf16[128,256]{1,0:T(8,128)(2,1)} %k_hbm.1, ...), custom_call_target="tpu_custom_call" | custom-call | tf_op jit(solution)/shard_map/attention/pallas_call | solution.py:632
  55.8 1.7 %results.1 = (bf16[128,512]{1,0:T(8,128)(2,1)}, bf16[256,128]{1,0:T(8,128)(2,1)}, bf16[128,256]{1,0:T(8,128)(2,1)}, bf16[128,256]{1,0:T(8,128)(2,1)}, bf16[128,256]{1,0:T(8,128)(2,1)}) custom-call(bf16[128,512]{1,0:T(8,128)(2,1)} %get-tuple-element.10.refs_0_, bf16[256,128]{1,0:T(8,128)(2,1)} %get-tuple-element.11.refs_1_, ...), custom_call_target="tpu_custom_call" | custom-call | tf_op jit(solution)/shard_map/results/pallas_call | solution.py:703

commit v5 on v4

--- a/solution.py
+++ b/solution.py
@@ -362,8 +362,8 @@
     absorb([(0, 0, 5), (0, 0, 6), (1, 0, 0)])
     take_sib(0, 3, 4)
     absorb([(0, 1, 3), (0, 1, 4)])
+    follow(3)
     advance(0, 3)
-    follow(3)
     absorb([(0, 0, 7), (1, 0, 1)])
     take_sib(0, 5, 6)
     absorb([(0, 1, 5), (0, 1, 6), (1, 1, 0)])

time: 57.8 us -> 57.8 us (level)
  no operation moved by 1% of the time
where the time goes in v5:
time: 57.8 us; the launch traced here: 57.7 us
  Pallas kernels  56.9 us (98%)
  between operations  0.8 us (1%)
    pallas_call x1, Pallas kernels, per_device(): pl.pallas_call(functools.partial(kernel, heads_n), out_shape=(jax.ShapeDt...  55.1 us
    pallas_call x1, Pallas kernels, per_device(): pl.pallas_call(hand_out, out_shape=tuple((jax.ShapeDtypeStruct(r.shape, r...  1.73 us

profile of v5, /device:TPU:4, one launch (start us, length us, event | category | flops | bytes accessed | tf_op | source)
XLA Modules:
  0.0 57.7 jit_solution(16776343446784592878)
XLA Ops:
  0.6 55.1 %attention.1 = (bf16[128,512]{1,0:T(8,128)(2,1)}, bf16[256,128]{1,0:T(8,128)(2,1)}, bf16[128,256]{1,0:T(8,128)(2,1)}, bf16[128,256]{1,0:T(8,128)(2,1)}, bf16[128,256]{1,0:T(8,128)(2,1)}) custom-call(s32[32]{0:T(128)} %len_ref.1, s32[32,32]{1,0:T(8,128)} %mask_ref.1, bf16[128,256]{1,0:T(8,128)(2,1)} %q_hbm.1, bf16[128,256]{1,0:T(8,128)(2,1)} %k_hbm.1, ...), custom_call_target="tpu_custom_call" | custom-call | tf_op jit(solution)/shard_map/attention/pallas_call | solution.py:632
  55.8 1.7 %results.1 = (bf16[128,512]{1,0:T(8,128)(2,1)}, bf16[256,128]{1,0:T(8,128)(2,1)}, bf16[128,256]{1,0:T(8,128)(2,1)}, bf16[128,256]{1,0:T(8,128)(2,1)}, bf16[128,256]{1,0:T(8,128)(2,1)}) custom-call(bf16[128,512]{1,0:T(8,128)(2,1)} %get-tuple-element.10.refs_0_, bf16[256,128]{1,0:T(8,128)(2,1)} %get-tuple-element.11.refs_1_, ...), custom_call_target="tpu_custom_call" | custom-call | tf_op jit(solution)/shard_map/results/pallas_call | solution.py:703

commit v6 on v5

--- a/solution.py
+++ b/solution.py
@@ -345,8 +345,6 @@
             sib(phase, slot).wait_recv()
 
     absorb([(0, 0, 0)])
-    pl.semaphore_wait(hello.at[0], 1)
-    pl.semaphore_signal(hello.at[1], inc=1, device_id=row_dev, device_id_type=MESH)
     advance(0, 0)
     follow(0)
     absorb([(0, 0, 1), (0, 0, 2)])
@@ -354,6 +352,8 @@
     absorb([(0, 1, 0)])
     advance(0, 1)
     follow(1)
+    pl.semaphore_wait(hello.at[0], 1)
+    pl.semaphore_signal(hello.at[1], inc=1, device_id=row_dev, device_id_type=MESH)
     absorb([(0, 0, 3), (0, 0, 4)])
     take_sib(0, 1, 2)
     absorb([(0, 1, 1), (0, 1, 2)])

time: 57.8 us -> 57.8 us (level)
  no operation moved by 1% of the time
where the time goes in v6:
time: 57.8 us; the launch traced here: 57.7 us
  Pallas kernels  56.9 us (98%)
  between operations  0.8 us (1%)
    pallas_call x1, Pallas kernels, per_device(): pl.pallas_call(functools.partial(kernel, heads_n), out_shape=(jax.ShapeDt...  55.1 us
    pallas_call x1, Pallas kernels, per_device(): pl.pallas_call(hand_out, out_shape=tuple((jax.ShapeDtypeStruct(r.shape, r...  1.73 us

profile of v6, /device:TPU:4, one launch (start us, length us, event | category | flops | bytes accessed | tf_op | source)
XLA Modules:
  0.0 57.7 jit_solution(11637140862211736236)
XLA Ops:
  0.6 55.1 %attention.1 = (bf16[128,512]{1,0:T(8,128)(2,1)}, bf16[256,128]{1,0:T(8,128)(2,1)}, bf16[128,256]{1,0:T(8,128)(2,1)}, bf16[128,256]{1,0:T(8,128)(2,1)}, bf16[128,256]{1,0:T(8,128)(2,1)}) custom-call(s32[32]{0:T(128)} %len_ref.1, s32[32,32]{1,0:T(8,128)} %mask_ref.1, bf16[128,256]{1,0:T(8,128)(2,1)} %q_hbm.1, bf16[128,256]{1,0:T(8,128)(2,1)} %k_hbm.1, ...), custom_call_target="tpu_custom_call" | custom-call | tf_op jit(solution)/shard_map/attention/pallas_call | solution.py:632
  55.8 1.7 %results.1 = (bf16[128,512]{1,0:T(8,128)(2,1)}, bf16[256,128]{1,0:T(8,128)(2,1)}, bf16[128,256]{1,0:T(8,128)(2,1)}, bf16[128,256]{1,0:T(8,128)(2,1)}, bf16[128,256]{1,0:T(8,128)(2,1)}) custom-call(bf16[128,512]{1,0:T(8,128)(2,1)} %get-tuple-element.10.refs_0_, bf16[256,128]{1,0:T(8,128)(2,1)} %get-tuple-element.11.refs_1_, ...), custom_call_target="tpu_custom_call" | custom-call | tf_op jit(solution)/shard_map/results/pallas_call | solution.py:703
